TPU v7x, 1024 devices: a whole 8x8x8 slice. The times are simulated.
1024 devices in a mesh: row: 16 (over z, core), col: 64 (over y, x).
Axes of the slice: x: 8, y: 8, z: 8, core: 2. Of those that a mesh axis runs over, the one named last changes fastest.
Arguments:
- features: float32 [131072, 128], P(('col', 'row')), may hold values from -6 to 6
- weight: float32 [128, 128], replicated, may hold values from -0.5 to 0.5
- adj_tiles: float32 [16, 64, 32, 128, 128], P('row', 'col'), may hold values from -0.0625 to 0.0625
- tile_row: int32 [16, 64, 32], P('row', 'col'), may hold values from 0 to 63
- tile_col: int32 [16, 64, 32], P('row', 'col'), may hold values from 0 to 15
- slot_count: int32 [16, 64], P('row', 'col'), may hold values from 4 to 32, as said below
- cotangent: float32 [131072, 128], P(('row', 'col')), may hold values from -6 to 6
Outputs:
- hidden: float32 [131072, 128], P(('row', 'col'))
- grad_input: float32 [131072, 128], P(('col', 'row'))
- grad_weight: float32 [128, 128], replicated
Inputs may be any that keep to these rules, and one draw needn't show every extreme that they name: `slot_count`: some device has all 32 slots live; the others have 32 divided by 1, 2, 4 or 8.
All inputs are finite; a program needn't handle non-finite values.
Results may differ from a plain program's by a relative error of at most 0.0003.
Values sent between devices are 32-bit elements; how exact they have to be, the bound alone decides.
A program may use at most 64 MiB of HBM per device.

v0:
```python
import jax
import jax.numpy as jnp
from jax import lax
from jax.sharding import PartitionSpec as P


def gelu_tanh(values):
    return jax.nn.gelu(values, approximate=True)


def tile_product(block, source, src_index, dst_index, live_count, dst_tiles, form):
    picked = source[src_index]
    product = jnp.einsum(form, block, picked, precision=lax.Precision.HIGHEST)
    slot_ids = jnp.arange(block.shape[0], dtype=jnp.int32)
    product = jnp.where((slot_ids < live_count)[:, None, None], product, jnp.float32(0.0))
    return jax.ops.segment_sum(product, dst_index, num_segments=dst_tiles)


def local(features, weight, adj_tiles, tile_row, tile_col, slot_count, cotangent):
    highest = lax.Precision.HIGHEST
    node_dev = features.shape[0]
    width = features.shape[1]
    tile_size = adj_tiles.shape[-1]
    row_tiles = node_dev * lax.axis_size("col") // tile_size
    col_tiles = node_dev * lax.axis_size("row") // tile_size
    block = adj_tiles[0, 0]
    rows = tile_row[0, 0]
    cols = tile_col[0, 0]
    live_count = slot_count[0, 0]
    projected = jnp.dot(features, weight, precision=highest, preferred_element_type=jnp.float32)
    column_block = lax.all_gather(projected, "row", axis=0, tiled=True)
    source = column_block.reshape(col_tiles, tile_size, width)
    partial_value = tile_product(block, source, cols, rows, live_count, row_tiles, "tij,tjf->tif")
    partial_value = partial_value.reshape(row_tiles * tile_size, width)
    owned = lax.psum_scatter(partial_value, "col", scatter_dimension=0, tiled=True)
    hidden, grad_fn = jax.vjp(gelu_tanh, owned)
    grad_pre = grad_fn(cotangent)[0]
    pre_rows = lax.all_gather(grad_pre, "col", axis=0, tiled=True)
    pre_source = pre_rows.reshape(row_tiles, tile_size, width)
    column_terms = tile_product(
        block, pre_source, rows, cols, live_count, col_tiles, "tji,tjf->tif"
    )
    column_terms = column_terms.reshape(col_tiles * tile_size, width)
    grad_projected = lax.psum_scatter(column_terms, "row", scatter_dimension=0, tiled=True)
    grad_input = jnp.dot(
        grad_projected, weight.T, precision=highest, preferred_element_type=jnp.float32
    )
    local_weight = jnp.dot(
        features.T, grad_projected, precision=highest, preferred_element_type=jnp.float32
    )
    grad_weight = lax.psum(local_weight, ("row", "col"))
    return (hidden, grad_input, grad_weight)


def solution(mesh):
    placed = (
        P(("col", "row"), None),
        P(),
        P("row", "col", None, None, None),
        P("row", "col", None),
        P("row", "col", None),
        P("row", "col"),
        P(("row", "col"), None),
    )
    return jax.shard_map(
        local,
        mesh=mesh,
        in_specs=placed,
        out_specs=(P(("row", "col"), None), P(("col", "row"), None), P()),
        check_vma=False,
    )
```

profile of v0, /device:TPU:1, one launch (start us, length us, event | category | flops | bytes accessed | tf_op | source)
XLA Modules:
  0.0 805.1 jit_solution(6032304325678606513)
XLA Ops:
  7.2 0.0 copy-start
  7.2 0.0 all-gather.3.cloned.1.call-start
  7.2 1.8 fusion.16
  9.1 0.0 all-gather.3.cloned.1.call-update
  9.1 0.0 reduce-scatter.3.cloned.1.call-start
  9.8 0.7 fusion.14
  10.5 59.3 %all-gather.3.cloned.1.call-done = f32[2048,128]{1,0:T(8,128)} async-done(((f32[128,128]{1,0:T(8,128)}), f32[2048,128]{1,0:T(8,128)}) %all-gather.3.cloned.1.call-update) | async-done | bytes 1048592 | tf_op jit(solution)/shard_map/all_gather | solution.py:31
  69.8 3.2 gather_fusion
  73.0 0.0 copy-done
  73.0 6.5 select_bitcast_fusion.1
  79.6 2.9 copy.14
  82.5 0.0 copy-start.5
  82.5 2.4 broadcast_in_dim.26
  85.0 0.0 copy-done.5
  85.0 6.9 scatter_fusion
  91.9 0.0 copy-start.4
  91.9 0.0 reduce-scatter.3.cloned.1.call-update
  91.9 0.0 all-gather.5.cloned.1.call-start
  92.0 244.7 %reduce-scatter.3.cloned.1.call-done = f32[128,128]{1,0:T(8,128)} async-done(((f32[8192,128]{1,0:T(8,128)}), f32[128,128]{1,0:T(8,128)}) %reduce-scatter.3.cloned.1.call-update) | async-done | bytes 65552 | tf_op jit(solution)/shard_map/reduce_scatter | solution.py:35
  336.6 0.0 copy-done.4
  336.6 1.5 fusion.13
  338.2 0.0 all-gather.5.cloned.1.call-update
  338.2 0.0 reduce-scatter.5.cloned.1.call-start
  338.3 95.7 %all-gather.5.cloned.1.call-done = f32[8192,128]{1,0:T(8,128)} async-done(((f32[128,128]{1,0:T(8,128)}), f32[8192,128]{1,0:T(8,128)}) %all-gather.5.cloned.1.call-update) | async-done | bytes 4194320 | tf_op jit(solution)/shard_map/all_gather | solution.py:38
  434.0 4.2 gather_fusion.1
  438.1 6.7 select_bitcast_fusion
  444.8 0.0 copy-start.6
  444.8 2.9 copy.16
  447.7 0.1 broadcast_in_dim.29
  447.8 0.0 copy-done.6
  447.9 0.0 copy-start.2
  447.9 0.0 copy-start.3
  447.9 4.7 scatter_fusion.1
  452.6 0.0 copy-start.1
  452.6 1.0 copy-done.1
  453.5 0.0 reduce-scatter.5.cloned.1.call-update
  453.5 0.0 all-reduce.2.cloned.1.call-start
  453.6 64.0 %reduce-scatter.5.cloned.1.call-done = f32[128,128]{1,0:T(8,128)} async-done(((f32[2048,128]{1,0:T(8,128)}), f32[128,128]{1,0:T(8,128)}) %reduce-scatter.5.cloned.1.call-update) | async-done | bytes 65552 | tf_op jit(solution)/shard_map/reduce_scatter | solution.py:44
  517.6 0.0 copy-done.2
  517.6 1.8 convolution_bitcast_fusion
  519.3 0.0 all-reduce.2.cloned.1.call-update
  519.3 0.0 copy-done.3
  519.3 1.7 fusion.17
  521.1 275.9 %all-reduce.2.cloned.1.call-done = f32[128,128]{0,1:T(8,128)} async-done(((f32[128,128]{0,1:T(8,128)}), f32[128,128]{0,1:T(8,128)}) %all-reduce.2.cloned.1.call-update) | async-done | bytes 65552 | tf_op jit(solution)/shard_map/psum | solution.py:51
  797.0 1.6 copy.17
  (4 shorter events, 0.0 us)
Async XLA Ops:
  7.2 65.9 %copy-start = (f32[1,1,32,128,128]{4,3,2,1,0:T(8,128)S(1)}, f32[1,1,32,128,128]{4,3,2,1,0:T(8,128)}, u32[]{:S(2)}) copy-start(f32[1,1,32,128,128]{4,3,2,1,0:T(8,128)} %param.9) | copy-start | bytes 6291460
  7.2 62.6 %all-gather.3.cloned.1.call-start = ((), (), s32[]{:S(2)}) async-start(), calls=%async_computation.2 | async-start | bytes 1114112 | tf_op jit(solution)/shard_map/all_gather | solution.py:31
  9.1 327.5 %reduce-scatter.3.cloned.1.call-start = ((), (), s32[]{:S(2)}) async-start(), calls=%async_computation.3 | async-start | bytes 4259840 | tf_op jit(solution)/shard_map/reduce_scatter | solution.py:35
  82.5 2.5 copy-start.5
  91.9 244.8 %copy-start.4 = (f32[128,128]{1,0:T(8,128)S(1)}, f32[128,128]{1,0:T(8,128)}, u32[]{:S(2)}) copy-start(f32[128,128]{1,0:T(8,128)} %param.13) | copy-start | bytes 196612
  91.9 342.0 %all-gather.5.cloned.1.call-start = ((), (), s32[]{:S(2)}) async-start(), calls=%async_computation.4 | async-start | bytes 4259840 | tf_op jit(solution)/shard_map/all_gather | solution.py:38
  338.2 179.3 %reduce-scatter.5.cloned.1.call-start = ((), (), s32[]{:S(2)}) async-start(), calls=%async_computation.5 | async-start | bytes 1114112 | tf_op jit(solution)/shard_map/reduce_scatter | solution.py:44
  444.8 3.0 copy-start.6
  447.9 69.7 %copy-start.2 = (f32[128,128]{1,0:T(8,128)S(1)}, f32[128,128]{1,0:T(8,128)}, u32[]{:S(2)}) copy-start(f32[128,128]{1,0:T(8,128)} %param.7) | copy-start | bytes 196612
  447.9 71.5 %copy-start.3 = (f32[128,128]{1,0:T(8,128)S(1)}, f32[128,128]{1,0:T(8,128)}, u32[]{:S(2)}) copy-start(f32[128,128]{1,0:T(8,128)} %param.8) | copy-start | bytes 196612
  452.6 1.0 copy-start.1
  453.5 343.4 %all-reduce.2.cloned.1.call-start = ((), (), s32[]{:S(2)}) async-start(), calls=%async_computation.6 | async-start | bytes 131072 | tf_op jit(solution)/shard_map/psum | solution.py:51
Sparse Core Ops, SparseCore 0:
  11.3 58.4 all-gather.2
  92.0 244.5 reduce-scatter.2
  342.2 91.7 all-gather.4
  453.7 63.8 reduce-scatter.4
  522.7 274.2 all-reduce.1
where the time goes:
time: 806 us; the launch traced here: 805 us
  waiting for transfers between devices  740 us (92%)
  matrix products  18.6 us (2%)
  local copies, waits for them, and re-layouts  18.4 us (2%)
  between operations  14.5 us (2%)
  other arithmetic  13.8 us (2%)
    psum x1, waiting for transfers between devices, local(): grad_weight = lax.psum(local_weight, ('row', 'col'))  276 us
    reduce_scatter x1, waiting for transfers between devices, local(): lax.psum_scatter(partial_value, 'col', scatter_dimension=0, tiled=True)  245 us
    all_gather x1, waiting for transfers between devices, local(): pre_rows = lax.all_gather(grad_pre, 'col', axis=0, tiled=True)  95.7 us
    reduce_scatter x1, waiting for transfers between devices, local(): lax.psum_scatter(column_terms, 'row', scatter_dimension=0, tiled=True)  64 us
    all_gather x1, waiting for transfers between devices, local(): column_block = lax.all_gather(projected, 'row', axis=0, tiled=True)  59.3 us
  transfers between devices with their start and end apart: 5, of which 5 were waited for; matrix products, arithmetic and copies ran while one was open for 0% of the time, Pallas kernels for 0%

commit v1 on v0

v1 whole, which is shorter than its diff:
```python
import functools
import jax
import jax.numpy as jnp
from jax import lax
from jax.experimental import pallas as pl
from jax.experimental.pallas import tpu as pltpu
from jax.sharding import PartitionSpec as P

MESH = pl.DeviceIdType.MESH
T = 128
NX = 8
F32 = jnp.float32
BF16 = jnp.bfloat16
VMEM = pl.BlockSpec(memory_space=pltpu.VMEM)
SMEM = pl.BlockSpec(memory_space=pltpu.SMEM)
LIMIT = 40 * 1024 * 1024


def split(value):
    high = value.astype(BF16)
    low = (value - high.astype(F32)).astype(BF16)
    return high, low


def dot3(left, right):
    lh, ll = split(left)
    rh, rl = split(right)
    return jnp.dot(
        jnp.concatenate([lh, ll, lh], axis=1),
        jnp.concatenate([rh, rh, rl], axis=0),
        preferred_element_type=F32,
    )


def steps_of(n, sign, half):
    return n // 2 if (sign > 0) == (half == 0) else n // 2 - 1


CHAINS = ((1, 0), (-1, 1), (1, 1), (-1, 0))


def wrap(index, n):
    return lax.rem(index + n, n)


def greet(peers):
    barrier = pltpu.get_barrier_semaphore()
    total = 0
    for count, device in peers:
        def one(k, carry, device=device):
            pl.semaphore_signal(barrier, inc=1, device_id=device(k), device_id_type=MESH)
            return carry
        lax.fori_loop(1, count + 1, one, 0)
        total += count
    pl.semaphore_wait(barrier, total)


def remote(src, dst, send, recv, device):
    return pltpu.make_async_remote_copy(
        src_ref=src, dst_ref=dst, send_sem=send, recv_sem=recv, device_id=device, device_id_type=MESH
    )


def z_gather_kernel(nz, x_ref, out_ref, ring_send, ring_recv, pair_send, pair_recv):
    row, col = lax.axis_index("row"), lax.axis_index("col")
    z, c = row // 2, lax.rem(row, 2)
    half_rows = T // 2
    ring = {s: (wrap(z + s, nz) * 2 + c, col) for s in (1, -1)}
    pair = (z * 2 + 1 - c, col)
    greet([(1, lambda k: ring[1]), (1, lambda k: ring[-1]), (1, lambda k: pair)])
    out_ref[z, c] = x_ref[...]

    def piece(zz, cc, half):
        return out_ref.at[zz, cc, pl.ds(half * half_rows, half_rows), :]

    def hop(i, t):
        sign, half = CHAINS[i]
        zz = wrap(z - sign * t, nz)
        return remote(piece(zz, c, half), piece(zz, c, half), ring_send.at[i, t], ring_recv.at[i, t], ring[sign])

    def arrival(i, t):
        sign, half = CHAINS[i]
        zz = wrap(z - sign * (t + 1), nz)
        return remote(piece(zz, c, half), piece(zz, c, half), ring_send.at[i, t], ring_recv.at[i, t], ring[sign])

    def share(i, t, cc):
        sign, half = CHAINS[i]
        zz = wrap(z - sign * (t + 1), nz)
        return remote(piece(zz, cc, half), piece(zz, cc, half), pair_send.at[i, t], pair_recv.at[i, t], pair)

    def own(cc):
        return remote(out_ref.at[z, cc], out_ref.at[z, cc], pair_send.at[4, 0], pair_recv.at[4, 0], pair)

    deep = [steps_of(nz, *chain) for chain in CHAINS]
    for i in range(4):
        hop(i, 0).start()
    own(c).start()
    for t in range(nz // 2):
        for i in range(4):
            if t < deep[i]:
                arrival(i, t).wait_recv()
                if t + 1 < deep[i]:
                    hop(i, t + 1).start()
                share(i, t, c).start()
    own(1 - c).wait_recv()
    for t in range(nz // 2):
        for i in range(4):
            if t < deep[i]:
                share(i, t, 1 - c).wait_recv()
    own(c).wait_send()
    for t in range(nz // 2):
        for i in range(4):
            if t < deep[i]:
                hop(i, t).wait_send()
                share(i, t, c).wait_send()


def z_gather(features, nz):
    return pl.pallas_call(
        functools.partial(z_gather_kernel, nz),
        out_shape=jax.ShapeDtypeStruct((nz, 2, T, T), F32),
        in_specs=[VMEM],
        out_specs=VMEM,
        scratch_shapes=[
            pltpu.SemaphoreType.DMA((4, nz // 2)),
            pltpu.SemaphoreType.DMA((4, nz // 2)),
            pltpu.SemaphoreType.DMA((5, nz // 2)),
            pltpu.SemaphoreType.DMA((5, nz // 2)),
        ],
        compiler_params=pltpu.CompilerParams(collective_id=0, has_side_effects=True, vmem_limit_bytes=LIMIT),
        name="z_gather",
    )(features)


GROUP = 4


def forward_kernel(rows, cols, count, adj, x, out, triple):
    out[...] = jnp.zeros_like(out)

    def prepare(c, carry):
        high, low = split(x[c])
        triple[c] = jnp.concatenate([high, high, low], axis=0)
        return carry

    lax.fori_loop(0, x.shape[0], prepare, 0)

    def group(g, carry):
        products = []
        for u in range(GROUP):
            s = g * GROUP + u
            high, low = split(adj[s])
            left = jnp.concatenate([high, low, high], axis=1)
            products.append(jnp.dot(left, triple[cols[s]], preferred_element_type=F32))
        for u in range(GROUP):
            r = rows[g * GROUP + u]
            out[r] = out[r] + products[u]
        return carry

    lax.fori_loop(0, count[0] // GROUP, group, 0)


def forward(rows, cols, count, adj, x, row_tiles):
    return pl.pallas_call(
        forward_kernel,
        out_shape=jax.ShapeDtypeStruct((row_tiles, T, T), F32),
        in_specs=[SMEM, SMEM, SMEM, VMEM, VMEM],
        out_specs=VMEM,
        scratch_shapes=[pltpu.VMEM((x.shape[0], 3 * T, T), BF16)],
        compiler_params=pltpu.CompilerParams(vmem_limit_bytes=LIMIT),
        name="forward_tiles",
    )(rows, cols, count, adj, x)


def backward_kernel(rows, cols, count, adj, g, out):
    out[...] = jnp.zeros_like(out)

    def group(i, carry):
        products = []
        for u in range(GROUP):
            s = i * GROUP + u
            products.append(dot3(g[rows[s]], adj[s]))
        for u in range(GROUP):
            c = cols[i * GROUP + u]
            out[c] = out[c] + products[u]
        return carry

    lax.fori_loop(0, count[0] // GROUP, group, 0)


def backward(rows, cols, count, adj, g, col_tiles):
    return pl.pallas_call(
        backward_kernel,
        out_shape=jax.ShapeDtypeStruct((col_tiles, T, T), F32),
        in_specs=[SMEM, SMEM, SMEM, VMEM, VMEM],
        out_specs=VMEM,
        compiler_params=pltpu.CompilerParams(vmem_limit_bytes=LIMIT),
        name="backward_tiles",
    )(rows, cols, count, adj, g)


def xy_kernel(
    ny, nx, nrow, partial, weight, cotangent, hidden, out, grad_weight,
    block, reduced, landed, send1, recv1, send2, recv2, sendA, recvA, sendB, recvB, sendC, recvC,
    lw, part_a, part_b, part_c, sendR, recvR, sendW, recvW,
):
    row, col = lax.axis_index("row"), lax.axis_index("col")
    y, x = col // nx, lax.rem(col, nx)
    size = (nx, ny)
    place = (x, y)
    quarter, half_rows = T // 4, T // 2
    wrows = T // nx

    def at_x(k):
        return (row, y * nx + wrap(x + k, nx))

    def at_y(k):
        return (row, wrap(y + k, ny) * nx + x)

    def at_row(k):
        return (lax.rem(row + k, nrow), col)

    along = (at_x, at_y)
    greet([(nx - 1, at_x), (ny - 1, at_y), (nrow - 1, at_row)])

    def tiles(ref, axis, where, start, count):
        if axis == 0:
            return ref.at[:, where, pl.ds(start, count), :]
        return ref.at[where, :, pl.ds(start, count), :]

    def first_row(axis, half):
        return axis * half_rows + half * quarter

    chains = [(axis, sign, half) for sign, half in CHAINS for axis in (0, 1)]
    deep = [steps_of(size[axis], sign, half) for axis, sign, half in chains]
    most = max(deep)

    def move(i, t):
        axis, sign, half = chains[i]
        if t == 0:
            src = tiles(partial, axis, wrap(place[axis] + sign * deep[i], size[axis]), first_row(axis, half), quarter)
        else:
            src = block.at[i, t - 1]
        return remote(src, block.at[i, t], send1.at[i, t], recv1.at[i, t], along[axis](sign))

    for i in range(len(chains)):
        move(i, 0).start()
    for t in range(1, most + 1):
        for i, (axis, sign, half) in enumerate(chains):
            if t < deep[i]:
                move(i, t - 1).wait_recv()
                mine = tiles(partial, axis, wrap(place[axis] + sign * (deep[i] - t), size[axis]), first_row(axis, half), quarter)
                block[i, t - 1] = block[i, t - 1] + mine[...]
                move(i, t).start()
    for half in (0, 1):
        for axis in (0, 1):
            plus, minus = chains.index((axis, 1, half)), chains.index((axis, -1, half))
            move(plus, deep[plus] - 1).wait_recv()
            move(minus, deep[minus] - 1).wait_recv()
            mine = tiles(partial, axis, place[axis], first_row(axis, half), quarter)
            reduced[axis, :, pl.ds(half * quarter, quarter), :] = (
                mine[...] + block[plus, deep[plus] - 1] + block[minus, deep[minus] - 1]
            )

    def part(axis, k):
        other = 1 - axis
        src = reduced.at[axis, wrap(place[other] + k, size[other])]
        return remote(src, landed.at[axis, place[other]], send2.at[axis, k], recv2.at[axis, k], along[other](k))

    def part_in(axis, k):
        other = 1 - axis
        slot = landed.at[axis, wrap(place[other] - k, size[other])]
        return remote(slot, slot, send2.at[axis, k], recv2.at[axis, k], along[other](-k))

    def loop(first, last, body):
        def step(k, carry):
            body(k)
            return carry
        lax.fori_loop(first, last, step, 0)

    for axis in (0, 1):
        loop(1, size[1 - axis], lambda k: part(axis, k).start())
    for axis in (0, 1):
        landed[axis, place[1 - axis]] = reduced[axis, place[1 - axis]]
    sums = []
    for axis in (0, 1):
        loop(1, size[1 - axis], lambda k: part_in(axis, k).wait_recv())
        total = landed[axis, 0]
        for k in range(1, size[1 - axis]):
            total = total + landed[axis, k]
        sums.append(total)
    summed = jnp.concatenate(sums, axis=0)

    value = dot3(summed, weight[...])
    scale = 0.7978845608028654
    t = jnp.tanh(scale * (value + 0.044715 * value * value * value))
    hidden[...] = 0.5 * value * (1.0 + t)
    slope = 0.5 * (1.0 + t) + 0.5 * value * (1.0 - t * t) * scale * (1.0 + 3.0 * 0.044715 * value * value)
    pre = cotangent[...] * slope
    out[y, x] = dot3(weight[...], pre.T)

    def spread(axis, k):
        other = 1 - axis
        ref = out.at[y, x, pl.ds(axis * half_rows, half_rows), :]
        return remote(ref, ref, sendA.at[axis, k], recvA.at[axis, k], along[other](k))

    def spread_in(axis, k):
        other = 1 - axis
        at = wrap(place[other] - k, size[other])
        ref = (out.at[at, x] if other == 1 else out.at[y, at]).at[pl.ds(axis * half_rows, half_rows), :]
        return remote(ref, ref, sendA.at[axis, k], recvA.at[axis, k], along[other](-k))

    def pass_on(axis, d, k):
        other = 1 - axis
        at = wrap(place[other] - k, size[other])
        ref = (out.at[at, x] if other == 1 else out.at[y, at]).at[pl.ds(axis * half_rows, half_rows), :]
        return remote(ref, ref, sendB.at[axis, d], recvB.at[axis, d], along[axis](1 - 2 * d))

    def passed(axis, d, sent):
        sign = 1 - 2 * d
        at = place[axis] if sent else wrap(place[axis] - sign, size[axis])
        ref = tiles(out, axis, at, axis * half_rows, half_rows)
        return remote(ref, ref, sendB.at[axis, d], recvB.at[axis, d], along[axis](sign))

    for axis in (0, 1):
        loop(1, size[1 - axis], lambda k: spread(axis, k).start())
        for d in (0, 1):
            pass_on(axis, d, 0).start()

    lw[...] = dot3(summed.T, pre)

    def weight_rows(k):
        return pl.ds(k * wrows, wrows)

    def scatter(k):
        at = wrap(x + k, nx)
        return remote(lw.at[weight_rows(at), :], part_a.at[x], sendR.at[0, k], recvR.at[0, k], at_x(k))

    def scatter_in(k):
        slot = part_a.at[wrap(x - k, nx)]
        return remote(slot, slot, sendR.at[0, k], recvR.at[0, k], at_x(-k))

    loop(1, nx, lambda k: scatter(k).start())
    part_a[x] = lw[weight_rows(x), :]

    def forward_tile(k):
        for axis in (0, 1):
            spread_in(axis, k).wait_recv()
            for d in (0, 1):
                pass_on(axis, d, k).start()

    loop(1, nx, forward_tile)

    def swap_y(k):
        return remote(part_b.at[y], part_b.at[y], sendR.at[1, k], recvR.at[1, k], at_y(k))

    def swap_y_in(k):
        slot = part_b.at[wrap(y - k, ny)]
        return remote(slot, slot, sendR.at[1, k], recvR.at[1, k], at_y(-k))

    def swap_row(k):
        return remote(part_c.at[row], part_c.at[row], sendW.at[k], recvW.at[k], at_row(k))

    def swap_row_in(k):
        slot = part_c.at[wrap(row - k, nrow)]
        return remote(slot, slot, sendW.at[k], recvW.at[k], at_row(nrow - k))

    def final(k):
        ref = grad_weight.at[weight_rows(x), :]
        return remote(ref, ref, sendR.at[2, k], recvR.at[2, k], at_x(k))

    def final_in(k):
        ref = grad_weight.at[weight_rows(wrap(x - k, nx)), :]
        return remote(ref, ref, sendR.at[2, k], recvR.at[2, k], at_x(-k))

    def add_up(slots, n):
        total = slots[0]
        for k in range(1, n):
            total = total + slots[k]
        return total

    def reduce_x():
        loop(1, nx, lambda k: scatter_in(k).wait_recv())
        part_b[y] = add_up(part_a, nx)
        loop(1, ny, lambda k: swap_y(k).start())

    def reduce_y():
        loop(1, ny, lambda k: swap_y_in(k).wait_recv())
        part_c[row] = add_up(part_b, ny)
        loop(1, nrow, lambda k: swap_row(k).start())

    def reduce_row():
        loop(1, nrow, lambda k: swap_row_in(k).wait_recv())
        grad_weight[weight_rows(x), :] = add_up(part_c, nrow)
        loop(1, nx, lambda k: final(k).start())

    between = {2: reduce_x, 3: reduce_y, 4: reduce_row}

    def relay(i, t, incoming):
        axis, sign, half = chains[i]
        at = wrap(place[axis] - sign * (t if incoming else t - 1), size[axis])
        ref = tiles(out, axis, at, first_row(axis, half), quarter)
        return remote(ref, ref, sendC.at[i, t], recvC.at[i, t], along[axis](sign))

    for t in range(2, most + 1):
        for i, (axis, sign, half) in enumerate(chains):
            if t == 2 and i in (0, 1, 2, 3):
                passed(axis, (1 - sign) // 2, False).wait_recv()
            if t <= deep[i]:
                if t > 2:
                    relay(i, t - 1, True).wait_recv()
                relay(i, t, False).start()
        between[t]()
    for i in range(len(chains)):
        relay(i, deep[i], True).wait_recv()
    loop(1, nx, lambda k: final_in(k).wait_recv())

    for i in range(len(chains)):
        for t in range(deep[i]):
            move(i, t).wait_send()
        for t in range(2, deep[i] + 1):
            relay(i, t, False).wait_send()
    for axis in (0, 1):
        loop(1, size[1 - axis], lambda k: part(axis, k).wait_send())
        loop(1, size[1 - axis], lambda k: spread(axis, k).wait_send())
        for d in (0, 1):
            passed(axis, d, True).wait_send()
    loop(1, nx, lambda k: scatter(k).wait_send())
    loop(1, ny, lambda k: swap_y(k).wait_send())
    loop(1, nrow, lambda k: swap_row(k).wait_send())
    loop(1, nx, lambda k: final(k).wait_send())


def xy(partial, weight, cotangent, ny, nx, nrow):
    partial = partial.reshape(ny, nx, T, T)
    most = max(nx, ny) // 2
    sem = pltpu.SemaphoreType.DMA
    big = max(nx, ny)
    return pl.pallas_call(
        functools.partial(xy_kernel, ny, nx, nrow),
        out_shape=(
            jax.ShapeDtypeStruct((T, T), F32),
            jax.ShapeDtypeStruct((ny, nx, T, T), F32),
            jax.ShapeDtypeStruct((T, T), F32),
        ),
        in_specs=[VMEM] * 3,
        out_specs=(VMEM,) * 3,
        scratch_shapes=[
            pltpu.VMEM((8, most, big, T // 4, T), F32),
            pltpu.VMEM((2, big, T // 2, T), F32),
            pltpu.VMEM((2, big, T // 2, T), F32),
            sem((8, most)), sem((8, most)),
            sem((2, big)), sem((2, big)),
            sem((2, big)), sem((2, big)),
            sem((2, 2)), sem((2, 2)),
            sem((8, most + 1)), sem((8, most + 1)),
            pltpu.VMEM((T, T), F32),
            pltpu.VMEM((nx, T // nx, T), F32),
            pltpu.VMEM((ny, T // nx, T), F32),
            pltpu.VMEM((nrow, T // nx, T), F32),
            sem((3, big)), sem((3, big)),
            sem((nrow,)), sem((nrow,)),
        ],
        compiler_params=pltpu.CompilerParams(collective_id=1, has_side_effects=True, vmem_limit_bytes=LIMIT),
        name="xy_exchange",
    )(partial, weight, cotangent)


def z_scatter_kernel(nz, part, out, other, block, pair_send, pair_recv, ring_send, ring_recv):
    row, col = lax.axis_index("row"), lax.axis_index("col")
    z, c = row // 2, lax.rem(row, 2)
    half_rows = T // 2
    ring = {s: (wrap(z + s, nz) * 2 + c, col) for s in (1, -1)}
    pair = (z * 2 + 1 - c, col)
    greet([(1, lambda k: ring[1]), (1, lambda k: ring[-1]), (1, lambda k: pair)])

    def give(off):
        zz = wrap(z + off, nz)
        return remote(part.at[zz, 1 - c], other.at[zz], pair_send.at[off % nz], pair_recv.at[off % nz], pair)

    far = nz // 2
    order = [far] + [s * k for k in range(far - 1, 0, -1) for s in (1, -1)] + [0]
    for off in order:
        give(off).start()
    taken = set()

    def take(off):
        if off % nz not in taken:
            taken.add(off % nz)
            give(off).wait_recv()

    def term(off, half):
        take(off)
        zz = wrap(z + off, nz)
        here = pl.ds(half * half_rows, half_rows)
        return part[zz, c, here, :] + other[zz, here, :]

    deep = [steps_of(nz, *chain) for chain in CHAINS]

    def move(i, t):
        return remote(block.at[i, t], block.at[i, t + 1], ring_send.at[i, t], ring_recv.at[i, t], ring[CHAINS[i][0]])

    for t in range(nz // 2):
        for i, (sign, half) in enumerate(CHAINS):
            if t < deep[i]:
                value = term(sign * (deep[i] - t), half)
                if t > 0:
                    move(i, t - 1).wait_recv()
                    value = value + block[i, t]
                block[i, t] = value
                move(i, t).start()
    rows = []
    for half in (0, 1):
        value = term(0, half)
        for i, chain in enumerate(CHAINS):
            if chain[1] == half:
                move(i, deep[i] - 1).wait_recv()
                value = value + block[i, deep[i]]
        rows.append(value)
    out[...] = jnp.concatenate(rows, axis=0).T
    for off in order:
        give(off).wait_send()
    for i in range(4):
        for t in range(deep[i]):
            move(i, t).wait_send()


def z_scatter(part, nz):
    sem = pltpu.SemaphoreType.DMA
    return pl.pallas_call(
        functools.partial(z_scatter_kernel, nz),
        out_shape=jax.ShapeDtypeStruct((T, T), F32),
        in_specs=[VMEM],
        out_specs=VMEM,
        scratch_shapes=[
            pltpu.VMEM((nz, T, T), F32),
            pltpu.VMEM((4, nz // 2 + 1, T // 2, T), F32),
            sem((nz,)), sem((nz,)),
            sem((4, nz // 2)), sem((4, nz // 2)),
        ],
        compiler_params=pltpu.CompilerParams(collective_id=2, has_side_effects=True, vmem_limit_bytes=LIMIT),
        name="z_scatter",
    )(part.reshape(nz, 2, T, T))


def local(nrow, ncol, features, weight, adj_tiles, tile_row, tile_col, slot_count, cotangent):
    nz, nx = nrow // 2, NX
    ny = ncol // nx
    rows, cols, count, adj = tile_row[0, 0], tile_col[0, 0], slot_count[0], adj_tiles[0, 0]
    x = z_gather(features, nz).reshape(nrow, T, T)
    partial = forward(rows, cols, count, adj, x, ncol)
    hidden, pre_rows, grad_weight = xy(partial, weight, cotangent, ny, nx, nrow)
    part = backward(rows, cols, count, adj, pre_rows.reshape(ncol, T, T), nrow)
    return hidden, z_scatter(part, nz), grad_weight


def solution(mesh):
    placed = (
        P(("col", "row"), None),
        P(),
        P("row", "col", None, None, None),
        P("row", "col", None),
        P("row", "col", None),
        P("row", "col"),
        P(("row", "col"), None),
    )
    return jax.shard_map(
        functools.partial(local, mesh.shape["row"], mesh.shape["col"]),
        mesh=mesh,
        in_specs=placed,
        out_specs=(P(("row", "col"), None), P(("col", "row"), None), P()),
        check_vma=False,
    )
```

time: 806 us -> 138 us (0.17)
  waiting for transfers between devices: 740 us -> 0 us
  Pallas kernels: 0 us -> 131 us
  matrix products: 18.6 us -> 0 us
  other arithmetic: 13.8 us -> 0 us
  between operations: 14.5 us -> 1.36 us
  local copies, waits for them, and re-layouts: 18.4 us -> 5.63 us
    reduce_scatter x2 -> x0, waiting for transfers between devices: 309 us -> none  [the longest x1 245 us: local(): lax.psum_scatter(partial_value, 'col', scatter_dimension=0, tiled=True)]
    psum x1 -> x0, waiting for transfers between devices: 276 us -> none  [local(): grad_weight = lax.psum(local_weight, ('row', 'col'))]
    all_gather x2 -> x0, waiting for transfers between devices: 155 us -> none  [the longest x1 95.7 us: local(): pre_rows = lax.all_gather(grad_pre, 'col', axis=0, tiled=True)]
    pallas_call x0 -> x5, Pallas kernels: none -> 131 us  [the longest x1 80.3 us: xy(): pl.pallas_call(functools.partial(xy_kernel, ny, nx, nrow), out_shape=(jax...]
    dot_general x5 -> x0, matrix products: 18.6 us -> none  [the longest x2 13.2 us: tile_product(): product = jnp.einsum(form, block, picked, precision=lax.Precision.HIGHEST)]
    scatter-add x2 -> x0, other arithmetic: 11.6 us -> none  [tile_product(): return jax.ops.segment_sum(product, dst_index, num_segments=dst_tiles)]
  transfers between devices with their start and end apart: 5 -> 0, of which waited for: 5 -> 0; matrix products, arithmetic and copies ran while one was open for 0% -> 0% of each run, Pallas kernels for 0% -> 0%
where the time goes in v1:
time: 138 us
  Pallas kernels  131 us (95%)
  local copies, waits for them, and re-layouts  5.63 us (4%)
    pallas_call x1, Pallas kernels, xy(): pl.pallas_call(functools.partial(xy_kernel, ny, nx, nrow), out_shape=(jax...  80.3 us
    pallas_call x1, Pallas kernels, z_gather(): pl.pallas_call(functools.partial(z_gather_kernel, nz), out_shape=jax.Shap...  31.2 us
    pallas_call x1, Pallas kernels, z_scatter(): pl.pallas_call(functools.partial(z_scatter_kernel, nz), out_shape=jax.Sha...  15.4 us
    unnamed x17, local copies, waits for them, and re-layouts  5.63 us

profile of v1, /device:TPU:1, one launch (start us, length us, event | category | flops | bytes accessed | tf_op | source)
XLA Modules:
  0.0 137.6 jit_solution(18322329753761977097)
XLA Ops:
  1.3 0.0 copy-start.4
  1.3 0.8 copy-done.4
  2.1 0.0 copy-start.2
  2.1 0.0 copy-start.3
  2.1 31.2 %z_gather.1 = f32[8,2,128,128]{3,2,1,0:T(8,128)S(1)} custom-call(f32[128,128]{1,0:T(8,128)S(1)} %copy-done.4), custom_call_target="tpu_custom_call" | custom-call | tf_op jit(solution)/shard_map/z_gather/pallas_call | solution.py:119
  33.3 0.0 copy-start
  33.3 1.6 %copy-done = f32[1,1,32,128,128]{4,3,2,1,0:T(8,128)S(1)} copy-done((f32[1,1,32,128,128]{4,3,2,1,0:T(8,128)S(1)}, f32[1,1,32,128,128]{4,3,2,1,0:T(8,128)}, u32[]{:S(2)}) %copy-start) | copy-done | bytes 2097176
  34.9 0.0 copy-start.5
  34.9 0.7 copy-done.5
  35.6 0.0 copy-start.6
  35.6 0.7 copy-done.6
  36.2 0.0 copy-start.1
  36.2 2.1 %forward_tiles.1 = f32[64,128,128]{2,1,0:T(8,128)S(1)} custom-call(s32[32]{0:T(128)S(1)} %bitcast.16, s32[32]{0:T(128)S(1)} %bitcast.18, s32[1]{0:T(128)} %bitcast.8.count, f32[32,128,128]{2,1,0:T(8,128)S(1)} %bitcast.11, f32[16,128,128]{2,1,0:T(8,128)S(1)} %bitcast.15), custom_call_target="tpu_custom_call" | custom-call | tf_op jit(solution)/shard_map/forward_tiles/pallas_call | solution.py:164
  38.3 0.0 copy-done.2
  38.3 0.0 copy-done.3
  38.3 80.3 %xy_exchange.1 = (f32[128,128]{1,0:T(8,128)S(1)}, f32[8,8,128,128]{3,2,1,0:T(8,128)S(1)}, f32[128,128]{1,0:T(8,128)S(1)}) custom-call(f32[8,8,128,128]{3,2,1,0:T(8,128)S(1)} %bitcast.10, f32[128,128]{1,0:T(8,128)S(1)} %copy-done.2, f32[128,128]{1,0:T(8,128)S(1)} %copy-done.3), custom_call_target="tpu_custom_call" | custom-call | tf_op jit(solution)/shard_map/xy_exchange/pallas_call | solution.py:439
  118.6 0.0 copy-done.1
  118.6 1.7 %backward_tiles.1 = f32[16,128,128]{2,1,0:T(8,128)S(1)} custom-call(s32[32]{0:T(128)S(1)} %bitcast.17, s32[32]{0:T(128)S(1)} %bitcast.19, s32[1]{0:T(128)} %bitcast.9.count, f32[32,128,128]{2,1,0:T(8,128)S(1)} %bitcast.12, f32[64,128,128]{2,1,0:T(8,128)S(1)} %bitcast.13), custom_call_target="tpu_custom_call" | custom-call | tf_op jit(solution)/shard_map/backward_tiles/pallas_call | solution.py:192
  120.3 15.4 %z_scatter.1 = f32[128,128]{1,0:T(8,128)S(1)} custom-call(f32[8,2,128,128]{3,2,1,0:T(8,128)S(1)} %bitcast.14), custom_call_target="tpu_custom_call" | custom-call | tf_op jit(solution)/shard_map/z_scatter/pallas_call | solution.py:530
  135.7 0.6 copy.14
  136.4 0.6 copy.15
  137.0 0.6 copy.16
Async XLA Ops:
  1.3 0.8 copy-start.4
  2.1 36.2 %copy-start.2 = (f32[128,128]{1,0:T(8,128)S(1)}, f32[128,128]{1,0:T(8,128)}, u32[]{:S(2)}) copy-start(f32[128,128]{1,0:T(8,128)} %weight.1) | copy-start | bytes 196612
  2.1 36.2 %copy-start.3 = (f32[128,128]{1,0:T(8,128)S(1)}, f32[128,128]{1,0:T(8,128)}, u32[]{:S(2)}) copy-start(f32[128,128]{1,0:T(8,128)} %cotangent.1) | copy-start | bytes 196612
  33.3 1.6 %copy-start = (f32[1,1,32,128,128]{4,3,2,1,0:T(8,128)S(1)}, f32[1,1,32,128,128]{4,3,2,1,0:T(8,128)}, u32[]{:S(2)}) copy-start(f32[1,1,32,128,128]{4,3,2,1,0:T(8,128)} %param.9) | copy-start | bytes 6291460
  34.9 0.7 copy-start.5
  35.6 0.7 copy-start.6
  36.2 82.4 %copy-start.1 = (f32[1,1,32,128,128]{4,3,2,1,0:T(8,128)S(1)}, f32[1,1,32,128,128]{4,3,2,1,0:T(8,128)}, u32[]{:S(2)}) copy-start(f32[1,1,32,128,128]{4,3,2,1,0:T(8,128)} %param.9) | copy-start | bytes 6291460

commit v2 on v0

v2 whole, which is shorter than its diff:
```python
import functools
import jax
import jax.numpy as jnp
from jax import lax
from jax.experimental import pallas as pl
from jax.experimental.pallas import tpu as pltpu
from jax.sharding import PartitionSpec as P

MESH = pl.DeviceIdType.MESH
T = 128
NX = 8
F32 = jnp.float32
BF16 = jnp.bfloat16
VMEM = pl.BlockSpec(memory_space=pltpu.VMEM)
SMEM = pl.BlockSpec(memory_space=pltpu.SMEM)
HBM = pl.BlockSpec(memory_space=pltpu.HBM)
MIB = 1024 * 1024


def split(value):
    high = value.astype(BF16)
    low = (value - high.astype(F32)).astype(BF16)
    return high, low


def dot3(left, right):
    lh, ll = split(left)
    rh, rl = split(right)
    return jnp.dot(
        jnp.concatenate([lh, ll, lh], axis=1),
        jnp.concatenate([rh, rh, rl], axis=0),
        preferred_element_type=F32,
    )


def wrap(index, n):
    return lax.rem(index + n, n)


def greet(peers):
    barrier = pltpu.get_barrier_semaphore()
    total = 0
    for count, device in peers:
        def one(k, carry, device=device):
            pl.semaphore_signal(barrier, inc=1, device_id=device(k), device_id_type=MESH)
            return carry
        lax.fori_loop(1, count + 1, one, 0)
        total += count
    pl.semaphore_wait(barrier, total)


def remote(src, dst, send, recv, device):
    return pltpu.make_async_remote_copy(
        src_ref=src, dst_ref=dst, send_sem=send, recv_sem=recv, device_id=device, device_id_type=MESH
    )


SIGNS = (1, -1)


def ring_peers(z, c, col, nz):
    return {k: (wrap(z + k, nz) * 2 + c, col) for k in (1, -1, 2, -2)}


def z_gather_kernel(
    nz, x_ref, adj, rows, cols, out_ref, adj_out, rows_out, cols_out,
    send, recv, relay_send, relay_recv, pair_send, pair_recv, fetch_sem,
):
    row, col = lax.axis_index("row"), lax.axis_index("col")
    z, c = row // 2, lax.rem(row, 2)
    half_rows = T // 2
    ring = ring_peers(z, c, col, nz)
    pair = (z * 2 + 1 - c, col)
    own = pltpu.make_async_copy(x_ref, out_ref.at[z, c], fetch_sem.at[0])
    own.start()
    fetches = [
        pltpu.make_async_copy(src, dst, fetch_sem.at[i])
        for i, (src, dst) in enumerate(((adj, adj_out), (rows, rows_out), (cols, cols_out)), 1)
    ]
    greet([(1, lambda k, to=to: to) for to in (*ring.values(), pair)])
    own.wait()

    def piece(off, cc, half):
        ref = out_ref.at[wrap(z + off, nz), cc]
        return ref if half is None else ref.at[pl.ds(half * half_rows, half_rows), :]

    def copy(ref, sems, i, j, to):
        return remote(ref, ref, sems[0].at[i, j], sems[1].at[i, j], to)

    first, second, shared = (send, recv), (relay_send, relay_recv), (pair_send, pair_recv)

    def far(d, half, off):
        return copy(piece(off, c, half), first, d, half, ring[2 * SIGNS[d]])

    def near(d, off):
        return copy(piece(off, c, None), first, d, 2, ring[SIGNS[d]])

    def third(d, half, off):
        return copy(piece(off, c, half), second, d, half, ring[SIGNS[d]])

    def fourth(d, off):
        return copy(piece(off, c, d), second, d, 2, ring[2 * SIGNS[d]])

    def share(i, off, cc):
        return copy(piece(off, cc, None), shared, 0, i, pair)

    for d in (0, 1):
        far(d, d, 0).start()
    for d in (0, 1):
        far(d, 1 - d, 0).start()
    for d in (0, 1):
        near(d, 0).start()
    share(0, 0, c).start()
    for fetch in fetches:
        fetch.start()
    for d in (0, 1):
        far(d, d, -2 * SIGNS[d]).wait_recv()
        fourth(d, -2 * SIGNS[d]).start()
        third(d, d, -2 * SIGNS[d]).start()
    for d in (0, 1):
        far(d, 1 - d, -2 * SIGNS[d]).wait_recv()
        third(d, 1 - d, -2 * SIGNS[d]).start()
        share(1 + d, -2 * SIGNS[d], c).start()
    for d in (0, 1):
        near(d, -SIGNS[d]).wait_recv()
        share(3 + d, -SIGNS[d], c).start()
    for d in (0, 1):
        for half in (0, 1):
            third(d, half, -3 * SIGNS[d]).wait_recv()
        share(5 + d, -3 * SIGNS[d], c).start()
    for d in (0, 1):
        fourth(d, -4 * SIGNS[d]).wait_recv()
    share(7, 4, c).start()
    offsets = (0, -2, 2, -1, 1, -3, 3, 4)
    for i, off in enumerate(offsets):
        share(i, off, 1 - c).wait_recv()
    for d in (0, 1):
        for half in (0, 1):
            far(d, half, 0).wait_send()
            third(d, half, -2 * SIGNS[d]).wait_send()
        near(d, 0).wait_send()
        fourth(d, -2 * SIGNS[d]).wait_send()
    for i, off in enumerate(offsets):
        share(i, off, c).wait_send()
    for fetch in fetches:
        fetch.wait()


def z_gather(features, adj, rows, cols, nz):
    sem = pltpu.SemaphoreType.DMA
    return pl.pallas_call(
        functools.partial(z_gather_kernel, nz),
        out_shape=(
            jax.ShapeDtypeStruct((nz, 2, T, T), F32),
            jax.ShapeDtypeStruct(adj.shape, F32),
            jax.ShapeDtypeStruct(rows.shape, jnp.int32),
            jax.ShapeDtypeStruct(cols.shape, jnp.int32),
        ),
        in_specs=[HBM] * 4,
        out_specs=(VMEM,) * 4,
        scratch_shapes=[
            sem((2, 3)), sem((2, 3)), sem((2, 3)), sem((2, 3)), sem((1, 8)), sem((1, 8)), sem((4,)),
        ],
        compiler_params=pltpu.CompilerParams(collective_id=0, has_side_effects=True, vmem_limit_bytes=6 * MIB),
        name="z_gather",
    )(features, adj, rows, cols)


GROUP = 4

OFFSETS = (4, 3, -3, 2, -2, 1, -1, 0)


def position(off):
    return jnp.where(off >= 4, 2 * (off - 4), 7 - 2 * off)


def relative(tile_row, col, nx, ny):
    ahead_y = lax.rem(tile_row // nx - col // nx + ny, ny)
    ahead_x = lax.rem(lax.rem(tile_row, nx) - lax.rem(col, nx) + nx, nx)
    return (0, ahead_x, position(ahead_y)), (1, ahead_y, position(ahead_x))


def forward_kernel(ny, nx, rows, cols, count, adj, x, out, triple):
    col = lax.axis_index("col")
    out[...] = jnp.zeros_like(out)

    def prepare(c, carry):
        high, low = split(x[c])
        triple[c] = jnp.concatenate([high, high, low], axis=0)
        return carry

    lax.fori_loop(0, x.shape[0], prepare, 0)

    def group(g, carry):
        products = []
        for u in range(GROUP):
            s = g * GROUP + u
            high, low = split(adj[s])
            left = jnp.concatenate([high, low, high], axis=1)
            products.append(jnp.dot(left, triple[cols[s]], preferred_element_type=F32))
        for u in range(GROUP):
            for half, at in enumerate(relative(rows[g * GROUP + u], col, nx, ny)):
                out[at] = out[at] + products[u][half * (T // 2) : (half + 1) * (T // 2)]
        return carry

    lax.fori_loop(0, count[0] // GROUP, group, 0)


def forward(rows, cols, count, adj, x, ny, nx):
    return pl.pallas_call(
        functools.partial(forward_kernel, ny, nx),
        out_shape=jax.ShapeDtypeStruct((2, 8, 8, T // 2, T), F32),
        in_specs=[SMEM, SMEM, SMEM, VMEM, VMEM],
        out_specs=VMEM,
        scratch_shapes=[pltpu.VMEM((x.shape[0], 3 * T, T), BF16)],
        compiler_params=pltpu.CompilerParams(vmem_limit_bytes=14 * MIB),
        name="forward_tiles",
    )(rows, cols, count, adj, x)


def backward_kernel(ny, nx, rows, cols, count, adj, g, hidden, grad_weight, out, hidden_out, grad_weight_out, sem):
    col = lax.axis_index("col")
    stores = [
        pltpu.make_async_copy(hidden, hidden_out, sem.at[0]),
        pltpu.make_async_copy(grad_weight, grad_weight_out, sem.at[1]),
    ]
    for store in stores:
        store.start()
    out[...] = jnp.zeros_like(out)

    def group(i, carry):
        products = []
        for u in range(GROUP):
            s = i * GROUP + u
            upper, lower = relative(rows[s], col, nx, ny)
            products.append(dot3(jnp.concatenate([g[upper], g[lower]], axis=0), adj[s]))
        for u in range(GROUP):
            c = cols[i * GROUP + u]
            out[c] = out[c] + products[u]
        return carry

    lax.fori_loop(0, count[0] // GROUP, group, 0)
    for store in stores:
        store.wait()


def backward(rows, cols, count, adj, g, hidden, grad_weight, col_tiles, ny, nx):
    return pl.pallas_call(
        functools.partial(backward_kernel, ny, nx),
        out_shape=(
            jax.ShapeDtypeStruct((col_tiles, T, T), F32),
            jax.ShapeDtypeStruct(hidden.shape, F32),
            jax.ShapeDtypeStruct(grad_weight.shape, F32),
        ),
        in_specs=[SMEM, SMEM, SMEM, VMEM, VMEM, VMEM, VMEM],
        out_specs=(VMEM, HBM, HBM),
        scratch_shapes=[pltpu.SemaphoreType.DMA((2,))],
        compiler_params=pltpu.CompilerParams(vmem_limit_bytes=12 * MIB),
        name="backward_tiles",
    )(rows, cols, count, adj, g, hidden, grad_weight)


FAR, NEAR = 0, 1


def group(g):
    return pl.ds(4 * g, 4)


def opposite(m):
    return OFFSETS.index(4 if m == 0 else -OFFSETS[m])


def xy_kernel(
    ny, nx, nrow, partial, weight, cotangent, hidden, out, grad_weight,
    first, begun, later, joined, landed, lw, part_a, part_b, part_c, w_tall, w_wide,
    send1, recv1, send2, recv2, sendA, recvA, sendB, recvB, sendR, recvR, sendW, recvW,
):
    row, col = lax.axis_index("row"), lax.axis_index("col")
    y, x = col // nx, lax.rem(col, nx)
    quarter, half_rows = T // 4, T // 2
    wrows = T // nx

    def at_x(k):
        return (row, y * nx + wrap(x + k, nx))

    def at_y(k):
        return (row, wrap(y + k, ny) * nx + x)

    def at_row(k):
        return (lax.rem(row + k, nrow), col)

    along = (at_x, at_y)
    neighbour = [{sign: along[axis](sign) for sign in SIGNS} for axis in (0, 1)]
    greet([(nx - 1, at_x), (ny - 1, at_y), (nrow - 1, at_row)])

    def loop(start, stop, body):
        def step(k, carry):
            body(k)
            return carry
        lax.fori_loop(start, stop, step, 0)

    both = ((0, 0), (1, 0), (0, 1), (1, 1))

    def quarter_of(d):
        return pl.ds(d * quarter, quarter)

    def move(axis, d, s, g):
        tiles = group(g)
        if s == 0:
            src, dst = partial.at[axis, 4, tiles, quarter_of(d), :], first.at[axis, d, tiles]
        elif s == 1:
            src, dst = begun.at[axis, d, tiles], later.at[axis, d, 0, tiles]
        else:
            src, dst = later.at[axis, d, s - 2, tiles], later.at[axis, d, s - 1, tiles]
        return remote(src, dst, send1.at[axis, d, s, g], recv1.at[axis, d, s, g], neighbour[axis][SIGNS[d]])

    def hop(axis, d, s, g):
        if s > 0:
            tiles = group(g)
            mine = partial[axis, (4 - s) * SIGNS[d] % 8, tiles]
            if s == 1:
                begun[axis, d, tiles] = mine
                move(axis, d, 0, g).wait_recv()
                begun[axis, d, tiles, quarter_of(d), :] = begun[axis, d, tiles, quarter_of(d), :] + first[axis, d, tiles]
            else:
                move(axis, d, s - 1, g).wait_recv()
                later[axis, d, s - 2, tiles] = later[axis, d, s - 2, tiles] + mine
        move(axis, d, s, g).start()

    def part(axis, m):
        return remote(
            joined.at[axis, m], landed.at[axis, m], send2.at[axis, m], recv2.at[axis, m], along[1 - axis](OFFSETS[m])
        )

    def finish(axis, g):
        tiles = group(g)
        for d in (0, 1):
            move(axis, d, 3, g).wait_recv()
        joined[axis, tiles] = partial[axis, 0, tiles] + later[axis, 0, 2, tiles] + later[axis, 1, 2, tiles]
        for m in range(4 * g, 4 * g + 4):
            if OFFSETS[m] != 0:
                part(axis, m).start()

    for s in range(4):
        for g in (FAR, NEAR):
            for axis, d in both:
                hop(axis, d, s, g)
        if s == 0:
            high, low = split(weight[...])
            w_tall[...] = jnp.concatenate([high, high, low], axis=0)
            w_wide[...] = jnp.concatenate([high, low, high], axis=1)
    for g in (FAR, NEAR):
        for axis in (0, 1):
            finish(axis, g)
    sums = []
    for axis in (0, 1):
        total = joined[axis, 7]
        for m in range(7):
            part(axis, m).wait_recv()
            total = total + landed[axis, m]
        sums.append(total)
    summed = jnp.concatenate(sums, axis=0)

    high, low = split(summed)
    value = jnp.dot(jnp.concatenate([high, low, high], axis=1), w_tall[...], preferred_element_type=F32)
    scale = 0.7978845608028654
    t = jnp.tanh(scale * (value + 0.044715 * value * value * value))
    slope = 0.5 * (1.0 + t) + 0.5 * value * (1.0 - t * t) * scale * (1.0 + 3.0 * 0.044715 * value * value)
    pre = cotangent[...] * slope
    high, low = split(pre)
    mixed = lax.dot_general(
        w_wide[...], jnp.concatenate([high, high, low], axis=1), (((1,), (1,)), ((), ())), preferred_element_type=F32
    )
    for axis in (0, 1):
        out[axis, 0, 7] = mixed[axis * half_rows : (axis + 1) * half_rows]

    def spread(axis, m):
        ref = out.at[axis, 0, 7]
        return remote(
            ref, out.at[axis, 0, opposite(m)], sendA.at[axis, m], recvA.at[axis, opposite(m)], along[1 - axis](OFFSETS[m])
        )

    def spread_in(axis, m):
        ref = out.at[axis, 0, m]
        return remote(ref, ref, sendA.at[axis, m], recvA.at[axis, m], along[1 - axis](OFFSETS[m]))

    def relay(axis, d, s, g):
        sign = SIGNS[d]
        tiles = group(g)
        rows = quarter_of(d) if s == 3 else slice(None)
        src = out.at[axis, -sign * s % 8, tiles, rows, :]
        dst = out.at[axis, -sign * (s + 1) % 8, tiles, rows, :]
        return remote(src, dst, sendB.at[axis, d, s, g], recvB.at[axis, d, s, g], neighbour[axis][sign])

    def hand_on(s, g):
        for axis, d in both:
            if s > 0:
                relay(axis, d, s - 1, g).wait_recv()
            relay(axis, d, s, g).start()

    for m in (6, 5, 4, 3, 2, 1, 0):
        for axis in (0, 1):
            spread(axis, m).start()

    hidden[...] = 0.5 * value * (1.0 + t)
    lw[...] = dot3(summed.T, pre)

    def weight_rows(k):
        return pl.ds(pl.multiple_of(k * wrows, wrows), wrows)

    def scatter(k):
        return remote(lw.at[weight_rows(wrap(x + k, nx)), :], part_a.at[x], sendR.at[0, k], recvR.at[0, k], at_x(k))

    def scatter_in(k):
        slot = part_a.at[wrap(x - k, nx)]
        return remote(slot, slot, sendR.at[0, k], recvR.at[0, k], at_x(k))

    def swap_y(k):
        return remote(part_b.at[y], part_b.at[y], sendR.at[1, k], recvR.at[1, k], at_y(k))

    def swap_y_in(k):
        slot = part_b.at[wrap(y - k, ny)]
        return remote(slot, slot, sendR.at[1, k], recvR.at[1, k], at_y(k))

    def swap_row(k):
        return remote(part_c.at[row], part_c.at[row], sendW.at[k], recvW.at[k], at_row(k))

    def swap_row_in(k):
        slot = part_c.at[wrap(row - k, nrow)]
        return remote(slot, slot, sendW.at[k], recvW.at[k], at_row(k))

    def final(k):
        ref = grad_weight.at[weight_rows(x), :]
        return remote(ref, ref, sendR.at[2, k], recvR.at[2, k], at_x(k))

    def final_in(k):
        ref = grad_weight.at[weight_rows(wrap(x - k, nx)), :]
        return remote(ref, ref, sendR.at[2, k], recvR.at[2, k], at_x(k))

    def add_up(slots, n):
        total = slots[0]
        for k in range(1, n):
            total = total + slots[k]
        return total

    part_a[x] = lw[weight_rows(x), :]
    loop(1, nx, lambda k: scatter(k).start())
    for m in (6, 5, 4):
        for axis in (0, 1):
            spread_in(axis, m).wait_recv()
    hand_on(0, NEAR)
    for m in (3, 2, 1, 0):
        for axis in (0, 1):
            spread_in(axis, m).wait_recv()
    hand_on(0, FAR)
    loop(1, nx, lambda k: scatter_in(k).wait_recv())
    part_b[y] = add_up(part_a, nx)
    loop(1, ny, lambda k: swap_y(k).start())
    hand_on(1, NEAR)
    hand_on(1, FAR)
    loop(1, ny, lambda k: swap_y_in(k).wait_recv())
    part_c[row] = add_up(part_b, ny)
    loop(1, nrow, lambda k: swap_row(k).start())
    hand_on(2, NEAR)
    hand_on(2, FAR)
    loop(1, nrow, lambda k: swap_row_in(k).wait_recv())
    grad_weight[weight_rows(x), :] = add_up(part_c, nrow)
    loop(1, nx, lambda k: final(k).start())
    hand_on(3, NEAR)
    hand_on(3, FAR)
    for g in (NEAR, FAR):
        for axis, d in both:
            relay(axis, d, 3, g).wait_recv()
    loop(1, nx, lambda k: final_in(k).wait_recv())

    for g in (FAR, NEAR):
        for axis, d in both:
            for s in range(4):
                move(axis, d, s, g).wait_send()
                relay(axis, d, s, g).wait_send()
    for axis in (0, 1):
        for m in range(7):
            part(axis, m).wait_send()
            spread(axis, m).wait_send()
    loop(1, nx, lambda k: scatter(k).wait_send())
    loop(1, ny, lambda k: swap_y(k).wait_send())
    loop(1, nrow, lambda k: swap_row(k).wait_send())
    loop(1, nx, lambda k: final(k).wait_send())


def xy(partial, weight, cotangent, ny, nx, nrow):
    sem = pltpu.SemaphoreType.DMA
    half, wrows = T // 2, T // nx
    return pl.pallas_call(
        functools.partial(xy_kernel, ny, nx, nrow),
        out_shape=(
            jax.ShapeDtypeStruct((T, T), F32),
            jax.ShapeDtypeStruct((2, 8, 8, half, T), F32),
            jax.ShapeDtypeStruct((T, T), F32),
        ),
        in_specs=[VMEM] * 3,
        out_specs=(VMEM,) * 3,
        scratch_shapes=[
            pltpu.VMEM((2, 2, 8, T // 4, T), F32),
            pltpu.VMEM((2, 2, 8, half, T), F32),
            pltpu.VMEM((2, 2, 3, 8, half, T), F32),
            pltpu.VMEM((2, 8, half, T), F32),
            pltpu.VMEM((2, 7, half, T), F32),
            pltpu.VMEM((T, T), F32),
            pltpu.VMEM((nx, wrows, T), F32),
            pltpu.VMEM((ny, wrows, T), F32),
            pltpu.VMEM((nrow, wrows, T), F32),
            pltpu.VMEM((3 * T, T), BF16),
            pltpu.VMEM((T, 3 * T), BF16),
            sem((2, 2, 4, 2)), sem((2, 2, 4, 2)),
            sem((2, 8)), sem((2, 8)),
            sem((2, 8)), sem((2, 8)),
            sem((2, 2, 4, 2)), sem((2, 2, 4, 2)),
            sem((3, 8)), sem((3, 8)),
            sem((nrow,)), sem((nrow,)),
        ],
        compiler_params=pltpu.CompilerParams(collective_id=1, has_side_effects=True, vmem_limit_bytes=20 * MIB),
        name="xy_exchange",
    )(partial, weight, cotangent)


def z_scatter_kernel(
    nz, part, out, other, acc, near_buf, relay_buf, third_buf, fourth_buf,
    pair_send, pair_recv, send, recv,
):
    row, col = lax.axis_index("row"), lax.axis_index("col")
    z, c = row // 2, lax.rem(row, 2)
    half_rows = T // 2
    ring = ring_peers(z, c, col, nz)
    pair = (z * 2 + 1 - c, col)
    greet([(1, lambda k, to=to: to) for to in (*ring.values(), pair)])

    def give(off):
        zz = wrap(z + off, nz)
        return remote(part.at[zz, 1 - c], other.at[zz], pair_send.at[off % nz], pair_recv.at[off % nz], pair)

    order = (4, 3, -3, 2, -2, 1, -1, 0)
    for off in order:
        give(off).start()

    def term(off):
        give(off).wait_recv()
        zz = wrap(z + off, nz)
        return part[zz, c] + other[zz]

    def copy(src, dst, d, kind, distance):
        return remote(src, dst, send.at[d, kind], recv.at[d, kind], ring[distance * SIGNS[d]])

    def fourth(d):
        return copy(acc.at[4, pl.ds(d * half_rows, half_rows), :], fourth_buf.at[d], d, 0, 2)

    def third(d):
        return copy(acc.at[2 + d], third_buf.at[d], d, 1, 1)

    def relay(d):
        return copy(acc.at[d], relay_buf.at[d], d, 2, 2)

    def near(d):
        return copy(acc.at[5 + d], near_buf.at[d], d, 3, 1)

    acc[4] = term(4)
    for d in (0, 1):
        fourth(d).start()
    for d in (0, 1):
        acc[2 + d] = term(3 * SIGNS[d])
        third(d).start()
    for d in (0, 1):
        acc[d] = term(2 * SIGNS[d])
    for d in (0, 1):
        acc[5 + d] = term(SIGNS[d])
        near(d).start()
    mine = term(0)
    for d in (0, 1):
        third(d).wait_recv()
        acc[d] = acc[d] + third_buf[d]
        fourth(d).wait_recv()
        here = pl.ds(d * half_rows, half_rows)
        acc[d, here, :] = acc[d, here, :] + fourth_buf[d]
        relay(d).start()
    for d in (0, 1):
        near(d).wait_recv()
        mine = mine + near_buf[d]
    for d in (0, 1):
        relay(d).wait_recv()
        mine = mine + relay_buf[d]
    out[...] = mine
    for off in order:
        give(off).wait_send()
    for d in (0, 1):
        fourth(d).wait_send()
        third(d).wait_send()
        relay(d).wait_send()
        near(d).wait_send()


def z_scatter(part, nz):
    sem = pltpu.SemaphoreType.DMA
    return pl.pallas_call(
        functools.partial(z_scatter_kernel, nz),
        out_shape=jax.ShapeDtypeStruct((T, T), F32),
        in_specs=[VMEM],
        out_specs=VMEM,
        scratch_shapes=[
            pltpu.VMEM((nz, T, T), F32),
            pltpu.VMEM((7, T, T), F32),
            pltpu.VMEM((2, T, T), F32),
            pltpu.VMEM((2, T, T), F32),
            pltpu.VMEM((2, T, T), F32),
            pltpu.VMEM((2, T // 2, T), F32),
            sem((nz,)), sem((nz,)),
            sem((2, 4)), sem((2, 4)),
        ],
        compiler_params=pltpu.CompilerParams(collective_id=2, has_side_effects=True, vmem_limit_bytes=6 * MIB),
        name="z_scatter",
    )(part.reshape(nz, 2, T, T))


def local(nrow, ncol, features, weight, adj_tiles, tile_row, tile_col, slot_count, cotangent):
    nz, nx = nrow // 2, NX
    ny = ncol // nx
    rows, cols, count, adj = tile_row[0, 0], tile_col[0, 0], slot_count[0], adj_tiles[0, 0]
    in_hbm = [pltpu.with_memory_space_constraint(a, pltpu.HBM) for a in (features, adj, rows, cols)]
    x, adj, rows, cols = z_gather(*in_hbm, nz)
    partial = forward(rows, cols, count, adj, x.reshape(nrow, T, T), ny, nx)
    hidden, pre_rows, grad_weight = xy(partial, weight, cotangent, ny, nx, nrow)
    part, hidden, grad_weight = backward(rows, cols, count, adj, pre_rows, hidden, grad_weight, nrow, ny, nx)
    return hidden, z_scatter(part, nz).T, grad_weight


def solution(mesh):
    placed = (
        P(("col", "row"), None),
        P(),
        P("row", "col", None, None, None),
        P("row", "col", None),
        P("row", "col", None),
        P("row", "col"),
        P(("row", "col"), None),
    )
    return jax.shard_map(
        functools.partial(local, mesh.shape["row"], mesh.shape["col"]),
        mesh=mesh,
        in_specs=placed,
        out_specs=(P(("row", "col"), None), P(("col", "row"), None), P()),
        check_vma=False,
    )
```

time: 806 us -> 123 us (0.15)
  waiting for transfers between devices: 740 us -> 0 us
  Pallas kernels: 0 us -> 120 us
  matrix products: 18.6 us -> 0 us
  local copies, waits for them, and re-layouts: 18.4 us -> 0.74 us
  other arithmetic: 13.8 us -> 0 us
  between operations: 14.5 us -> 1.35 us
    reduce_scatter x2 -> x0, waiting for transfers between devices: 309 us -> none  [the longest x1 245 us: local(): lax.psum_scatter(partial_value, 'col', scatter_dimension=0, tiled=True)]
    psum x1 -> x0, waiting for transfers between devices: 276 us -> none  [local(): grad_weight = lax.psum(local_weight, ('row', 'col'))]
    all_gather x2 -> x0, waiting for transfers between devices: 155 us -> none  [the longest x1 95.7 us: local(): pre_rows = lax.all_gather(grad_pre, 'col', axis=0, tiled=True)]
    pallas_call x0 -> x5, Pallas kernels: none -> 120 us  [the longest x1 74.5 us: xy(): pl.pallas_call(functools.partial(xy_kernel, ny, nx, nrow), out_shape=(jax...]
    dot_general x5 -> x0, matrix products: 18.6 us -> none  [the longest x2 13.2 us: tile_product(): product = jnp.einsum(form, block, picked, precision=lax.Precision.HIGHEST)]
    scatter-add x2 -> x0, other arithmetic: 11.6 us -> none  [tile_product(): return jax.ops.segment_sum(product, dst_index, num_segments=dst_tiles)]
  transfers between devices with their start and end apart: 5 -> 0, of which waited for: 5 -> 0; matrix products, arithmetic and copies ran while one was open for 0% -> 0% of each run, Pallas kernels for 0% -> 0%
where the time goes in v2:
time: 123 us; the launch traced here: 122 us
  Pallas kernels  120 us (98%)
  between operations  1.35 us (1%)
    pallas_call x1, Pallas kernels, xy(): pl.pallas_call(functools.partial(xy_kernel, ny, nx, nrow), out_shape=(jax...  74.5 us
    pallas_call x1, Pallas kernels, z_gather(): pl.pallas_call(functools.partial(z_gather_kernel, nz), out_shape=(jax.Sha...  27.6 us
    pallas_call x1, Pallas kernels, z_scatter(): pl.pallas_call(functools.partial(z_scatter_kernel, nz), out_shape=jax.Sha...  15.6 us

profile of v2, /device:TPU:1, one launch (start us, length us, event | category | flops | bytes accessed | tf_op | source)
XLA Modules:
  0.0 122.2 jit_solution(18320330953038149018)
XLA Ops:
  1.3 27.6 %z_gather.1 = (f32[8,2,128,128]{3,2,1,0:T(8,128)S(1)}, f32[32,128,128]{2,1,0:T(8,128)S(1)}, s32[32]{0:T(128)S(1)}, s32[32]{0:T(128)S(1)}) custom-call(f32[128,128]{1,0:T(8,128)} %x_ref.1, f32[32,128,128]{2,1,0:T(8,128)} %bitcast.12, s32[32]{0:T(128)} %bitcast.13, s32[32]{0:T(128)} %bitcast.14), custom_call_target="tpu_custom_call" | custom-call | tf_op jit(solution)/shard_map/z_gather/pallas_call | solution.py:151
  28.9 0.0 copy-start
  28.9 0.0 copy-start.1
  28.9 1.3 %forward_tiles.1.partial = f32[2,8,8,64,128]{4,3,2,1,0:T(8,128)S(1)} custom-call(s32[32]{0:T(128)S(1)} %get-tuple-element.13.rows, s32[32]{0:T(128)S(1)} %get-tuple-element.14.cols, s32[1]{0:T(128)} %bitcast.7.count, f32[32,128,128]{2,1,0:T(8,128)S(1)} %get-tuple-element.15.adj, f32[16,128,128]{2,1,0:T(8,128)S(1)} %bitcast.10), custom_call_target="tpu_custom_call" | custom-call | tf_op jit(solution)/shard_map/forward_tiles/pallas_call | solution.py:211
  30.2 0.0 copy-done
  30.2 0.0 copy-done.1
  30.2 74.5 %xy_exchange.1 = (f32[128,128]{1,0:T(8,128)S(1)}, f32[2,8,8,64,128]{4,3,2,1,0:T(8,128)S(1)}, f32[128,128]{1,0:T(8,128)S(1)}) custom-call(f32[2,8,8,64,128]{4,3,2,1,0:T(8,128)S(1)} %forward_tiles.1.partial, f32[128,128]{1,0:T(8,128)S(1)} %copy-done, f32[128,128]{1,0:T(8,128)S(1)} %copy-done.1), custom_call_target="tpu_custom_call" | custom-call | tf_op jit(solution)/shard_map/xy_exchange/pallas_call | solution.py:496
  104.7 1.2 backward_tiles.1
  105.9 15.6 %z_scatter.1 = f32[128,128]{1,0:T(8,128)S(1)} custom-call(f32[8,2,128,128]{3,2,1,0:T(8,128)S(1)} %bitcast.9), custom_call_target="tpu_custom_call" | custom-call | tf_op jit(solution)/shard_map/z_scatter/pallas_call | solution.py:605
  121.5 0.7 copy.10
Async XLA Ops:
  28.9 1.3 %copy-start = (f32[128,128]{1,0:T(8,128)S(1)}, f32[128,128]{1,0:T(8,128)}, u32[]{:S(2)}) copy-start(f32[128,128]{1,0:T(8,128)} %weight.1) | copy-start | bytes 196612
  28.9 1.3 %copy-start.1 = (f32[128,128]{1,0:T(8,128)S(1)}, f32[128,128]{1,0:T(8,128)}, u32[]{:S(2)}) copy-start(f32[128,128]{1,0:T(8,128)} %cotangent.1) | copy-start | bytes 196612

commit v3 on v2

--- a/solution.py
+++ b/solution.py
@@ -166,7 +166,7 @@
     )(features, adj, rows, cols)
 
 
-GROUP = 4
+GROUP = 8
 
 OFFSETS = (4, 3, -3, 2, -2, 1, -1, 0)
 
@@ -198,13 +198,14 @@
             s = g * GROUP + u
             high, low = split(adj[s])
             left = jnp.concatenate([high, low, high], axis=1)
-            products.append(jnp.dot(left, triple[cols[s]], preferred_element_type=F32))
+            product = jnp.dot(left, triple[cols[s]], preferred_element_type=F32)
+            products.append(jnp.where(s < count[0], product, 0.0))
         for u in range(GROUP):
             for half, at in enumerate(relative(rows[g * GROUP + u], col, nx, ny)):
                 out[at] = out[at] + products[u][half * (T // 2) : (half + 1) * (T // 2)]
         return carry
 
-    lax.fori_loop(0, count[0] // GROUP, group, 0)
+    lax.fori_loop(0, (count[0] + GROUP - 1) // GROUP, group, 0)
 
 
 def forward(rows, cols, count, adj, x, ny, nx):
@@ -234,13 +235,14 @@
         for u in range(GROUP):
             s = i * GROUP + u
             upper, lower = relative(rows[s], col, nx, ny)
-            products.append(dot3(jnp.concatenate([g[upper], g[lower]], axis=0), adj[s]))
+            product = dot3(jnp.concatenate([g[upper], g[lower]], axis=0), adj[s])
+            products.append(jnp.where(s < count[0], product, 0.0))
         for u in range(GROUP):
             c = cols[i * GROUP + u]
             out[c] = out[c] + products[u]
         return carry
 
-    lax.fori_loop(0, count[0] // GROUP, group, 0)
+    lax.fori_loop(0, (count[0] + GROUP - 1) // GROUP, group, 0)
     for store in stores:
         store.wait()
 

time: 123 us -> 121 us (0.984)
  Pallas kernels: 120 us -> 118 us
    pallas_call x1, Pallas kernels: 15.6 us -> 14.3 us  [z_scatter(): pl.pallas_call(functools.partial(z_scatter_kernel, nz), out_shape=jax.Sha...]
where the time goes in v3:
time: 121 us
  Pallas kernels  118 us (98%)
  between operations  1.35 us (1%)
    pallas_call x1, Pallas kernels, xy(): pl.pallas_call(functools.partial(xy_kernel, ny, nx, nrow), out_shape=(jax...  74 us
    pallas_call x1, Pallas kernels, z_gather(): pl.pallas_call(functools.partial(z_gather_kernel, nz), out_shape=(jax.Sha...  27.6 us
    pallas_call x1, Pallas kernels, z_scatter(): pl.pallas_call(functools.partial(z_scatter_kernel, nz), out_shape=jax.Sha...  14.3 us

profile of v3, /device:TPU:1, one launch (start us, length us, event | category | flops | bytes accessed | tf_op | source)
XLA Modules:
  0.0 120.6 jit_solution(17044912103877167531)
XLA Ops:
  1.3 27.6 %z_gather.1 = (f32[8,2,128,128]{3,2,1,0:T(8,128)S(1)}, f32[32,128,128]{2,1,0:T(8,128)S(1)}, s32[32]{0:T(128)S(1)}, s32[32]{0:T(128)S(1)}) custom-call(f32[128,128]{1,0:T(8,128)} %x_ref.1, f32[32,128,128]{2,1,0:T(8,128)} %bitcast.12, s32[32]{0:T(128)} %bitcast.13, s32[32]{0:T(128)} %bitcast.14), custom_call_target="tpu_custom_call" | custom-call | tf_op jit(solution)/shard_map/z_gather/pallas_call | solution.py:151
  28.9 0.0 copy-start
  28.9 0.0 copy-start.1
  28.9 1.4 %forward_tiles.1.partial = f32[2,8,8,64,128]{4,3,2,1,0:T(8,128)S(1)} custom-call(s32[32]{0:T(128)S(1)} %get-tuple-element.13.rows, s32[32]{0:T(128)S(1)} %get-tuple-element.14.cols, s32[1]{0:T(128)} %bitcast.7.count, f32[32,128,128]{2,1,0:T(8,128)S(1)} %get-tuple-element.15.adj, f32[16,128,128]{2,1,0:T(8,128)S(1)} %bitcast.10), custom_call_target="tpu_custom_call" | custom-call | tf_op jit(solution)/shard_map/forward_tiles/pallas_call | solution.py:212
  30.3 0.0 copy-done
  30.3 0.0 copy-done.1
  30.3 74.0 %xy_exchange.1 = (f32[128,128]{1,0:T(8,128)S(1)}, f32[2,8,8,64,128]{4,3,2,1,0:T(8,128)S(1)}, f32[128,128]{1,0:T(8,128)S(1)}) custom-call(f32[2,8,8,64,128]{4,3,2,1,0:T(8,128)S(1)} %forward_tiles.1.partial, f32[128,128]{1,0:T(8,128)S(1)} %copy-done, f32[128,128]{1,0:T(8,128)S(1)} %copy-done.1), custom_call_target="tpu_custom_call" | custom-call | tf_op jit(solution)/shard_map/xy_exchange/pallas_call | solution.py:498
  104.3 1.2 %backward_tiles.1 = (f32[16,128,128]{2,1,0:T(8,128)S(1)}, f32[128,128]{1,0:T(8,128)}, f32[128,128]{1,0:T(8,128)}) custom-call(s32[32]{0:T(128)S(1)} %get-tuple-element.13.rows, s32[32]{0:T(128)S(1)} %get-tuple-element.14.cols, s32[1]{0:T(128)} %bitcast.8.count, f32[32,128,128]{2,1,0:T(8,128)S(1)} %get-tuple-element.15.adj, ...), custom_call_target="tpu_custom_call" | custom-call | tf_op jit(solution)/shard_map/backward_tiles/pallas_call | solution.py:251
  105.5 14.3 %z_scatter.1 = f32[128,128]{1,0:T(8,128)S(1)} custom-call(f32[8,2,128,128]{3,2,1,0:T(8,128)S(1)} %bitcast.9), custom_call_target="tpu_custom_call" | custom-call | tf_op jit(solution)/shard_map/z_scatter/pallas_call | solution.py:607
  119.8 0.7 copy.10
Async XLA Ops:
  28.9 1.4 %copy-start = (f32[128,128]{1,0:T(8,128)S(1)}, f32[128,128]{1,0:T(8,128)}, u32[]{:S(2)}) copy-start(f32[128,128]{1,0:T(8,128)} %weight.1) | copy-start | bytes 196612
  28.9 1.4 %copy-start.1 = (f32[128,128]{1,0:T(8,128)S(1)}, f32[128,128]{1,0:T(8,128)}, u32[]{:S(2)}) copy-start(f32[128,128]{1,0:T(8,128)} %cotangent.1) | copy-start | bytes 196612
